TPU v7x, 256 devices: a whole 4x4x8 slice. The times are simulated.
256 devices in a mesh: pair: 8 (over x, core), slab: 32 (over y, z).
Axes of the slice: x: 4, y: 4, z: 8, core: 2. Of those that a mesh axis runs over, the one named last changes fastest.
Arguments:
- amplitudes: bfloat16 [1024, 640, 640], P('pair', 'slab'), may hold values from -6 to 6
- integrals: bfloat16 [640, 640, 1024], P('slab', 'pair'), may hold values from -0.013671875 to 0.013671875
- block_map: int32 [10, 10], replicated, may hold values from 0 to 1, as said below
- driver: bfloat16 [1024, 1024], P(('pair', 'slab')), may hold values from -6 to 6
Outputs:
- residual: float32 [1024, 1024], P(('pair', 'slab'))
Inputs may be any that keep to these rules, and one draw needn't show every extreme that they name: Each block carries an irreducible-representation label of 0 to 7; block_map[c, d] is 1 exactly where the labels of blocks c and d combine (bitwise exclusive or) to the window's label, which is not 0.
All inputs are finite; a program needn't handle non-finite values.
Results may differ from a plain program's by a relative error of at most 0.0003.
Values may be sent and summed in bfloat16 or wider, within the bound.
A program may use at most 128 MiB of HBM per device.

v0:
```python
import jax
import jax.numpy as jnp
from jax import lax
from jax.sharding import PartitionSpec as P

BLK = 64


def allowed_block(table, c_start, c_width, d_start, d_width):
    n_blocks = table.shape[0]
    c_onehot = ((c_start + jnp.arange(c_width)) // BLK)[:, None] == jnp.arange(n_blocks)[None, :]
    d_onehot = ((d_start + jnp.arange(d_width)) // BLK)[:, None] == jnp.arange(n_blocks)[None, :]
    inner = jnp.dot(c_onehot.astype(jnp.float32), table)
    return jnp.dot(inner, d_onehot.astype(jnp.float32).T).astype(jnp.bfloat16)


def on_device(amplitudes, integrals, block_map, driver):
    c_width = amplitudes.shape[1]
    c_start = lax.axis_index("slab") * c_width
    table = block_map.astype(jnp.float32)
    window = integrals.shape[2]
    swapped = lax.all_to_all(amplitudes, "pair", split_axis=2, concat_axis=0, tiled=True)
    d_width = swapped.shape[2]
    d_start = lax.axis_index("pair") * d_width
    allowed = allowed_block(table, c_start, c_width, d_start, d_width)
    masked = (integrals * allowed[:, :, None]).reshape(c_width * d_width, window)
    flat_amps = swapped.reshape(swapped.shape[0], c_width * d_width)
    ladder = lax.psum_scatter(
        jnp.dot(flat_amps, masked, preferred_element_type=jnp.float32),
        ("pair", "slab"),
        scatter_dimension=0,
        tiled=True,
    )
    return driver.astype(jnp.float32) + ladder


def solution(mesh):
    placed = (P("pair", "slab", None), P("slab", "pair", None), P(), P(("pair", "slab"), None))
    return jax.shard_map(
        on_device, mesh=mesh, in_specs=placed, out_specs=P(("pair", "slab"), None), check_vma=False
    )
```

profile of v0, /device:TPU:2, one launch (start us, length us, event | category | flops | bytes accessed | tf_op | source)
XLA Modules:
  0.0 353.3 jit_solution(6857202486924132799)
XLA Ops:
  6.5 6.2 %copy.16 = bf16[128,20,640]{0,1,2:T(8,128)(2,1)} copy(bf16[128,20,640]{2,0,1:T(8,128)(2,1)} %param.4) | data formatting | bytes 6553600 | tf_op args[0]
  12.8 0.0 copy-start.3
  12.8 0.0 copy-start
  12.8 6.9 %all-to-all-start = ((bf16[128,20,640]{0,1,2:T(8,128)(2,1)}), bf16[128,20,640]{0,1,2:T(8,128)(2,1)}, u32[]{:S(2)}, u32[]{:S(2)}) async-start(bf16[128,20,640]{0,1,2:T(8,128)(2,1)} %copy.16), calls=%async_computation | async-start | bytes 7864320 | tf_op jit(solution)/shard_map/all_to_all | solution.py:22
  19.7 0.0 all-reduce.3.cloned.1.call-start
  19.7 0.0 copy-done.3
  19.7 0.4 convolution_convert_fusion
  20.1 0.0 copy-done
  20.1 2.1 broadcast_multiply_fusion
  22.2 43.0 %all-to-all-done = bf16[128,20,640]{0,1,2:T(8,128)(2,1)} async-done(((bf16[128,20,640]{0,1,2:T(8,128)(2,1)}), bf16[128,20,640]{0,1,2:T(8,128)(2,1)}, u32[]{:S(2)}, u32[]{:S(2)}) %all-to-all-start) | async-done | bytes 3276832 | tf_op jit(solution)/shard_map/all_to_all | solution.py:22
  65.2 0.0 copy-start.1
  65.2 4.4 %copy.18 = bf16[8,128,20,80]{1,0,3,2:T(8,128)(2,1)S(1)} copy(bf16[8,128,20,80]{1,2,3,0:T(8,128)(2,1)} %bitcast.3) | data formatting | bytes 6553600 | tf_op jit(solution)/shard_map/all_to_all | solution.py:22
  69.6 0.0 copy-done.1
  69.6 5.7 %fusion.3 = f32[1024,1024]{0,1:T(8,128)} fusion(bf16[1600,1024]{1,0:T(8,128)(2,1)S(1)} %bitcast.19, bf16[200,8,8,128]{3,2,1,0:T(8,128)(2,1)S(1)} %bitcast.18), kind=kOutput, calls=%fused_computation.3 | convolution fusion | flops 3355443200 | bytes 10747904 | tf_op jit(solution)/shard_map/dot_general | solution.py:29
  75.3 0.0 copy-start.2
  75.3 0.0 all-reduce.3.cloned.1.call-update
  75.4 269.0 %all-reduce.3.cloned.1.call-done = f32[1024,1024]{0,1:T(8,128)} async-done(((f32[1024,1024]{0,1:T(8,128)}), f32[1024,1024]{0,1:T(8,128)}) %all-reduce.3.cloned.1.call-update) | async-done | bytes 4194320
  344.4 1.2 constant_dynamic-slice_fusion
  345.6 0.2 copy.19
  345.8 0.0 copy-done.2
  345.8 0.6 convert_add_fusion
  (2 shorter events, 0.0 us)
Async XLA Ops:
  12.8 7.0 %copy-start.3 = (s32[10,10]{1,0:T(8,128)S(1)}, s32[10,10]{1,0:T(8,128)}, u32[]{:S(2)}) copy-start(s32[10,10]{1,0:T(8,128)} %param.6) | copy-start | bytes 1204
  12.8 7.4 %copy-start = (bf16[20,80,1024]{2,1,0:T(8,128)(2,1)S(1)}, bf16[20,80,1024]{2,1,0:T(8,128)(2,1)}, u32[]{:S(2)}) copy-start(bf16[20,80,1024]{2,1,0:T(8,128)(2,1)} %param.5) | copy-start | bytes 9830404
  12.8 52.5 %all-to-all-start = ((bf16[128,20,640]{0,1,2:T(8,128)(2,1)}), bf16[128,20,640]{0,1,2:T(8,128)(2,1)}, u32[]{:S(2)}, u32[]{:S(2)}) async-start(bf16[128,20,640]{0,1,2:T(8,128)(2,1)} %copy.16), calls=%async_computation | async-start | bytes 7864320 | tf_op jit(solution)/shard_map/all_to_all | solution.py:22
  19.7 324.7 %all-reduce.3.cloned.1.call-start = ((), (), s32[]{:S(2)}) async-start(), calls=%async_computation.1 | async-start | bytes 8388608
  65.2 4.4 %copy-start.1 = (bf16[20,80,1024]{2,1,0:T(8,128)(2,1)S(1)}, bf16[20,80,1024]{2,1,0:T(8,128)(2,1)}, u32[]{:S(2)}) copy-start(bf16[20,80,1024]{2,1,0:T(8,128)(2,1)} %broadcast_multiply_fusion) | copy-start | bytes 9830404
  75.3 270.5 %copy-start.2 = (bf16[4,1024]{1,0:T(4,128)(2,1)S(1)}, bf16[4,1024]{1,0:T(4,128)(2,1)}, u32[]{:S(2)}) copy-start(bf16[4,1024]{1,0:T(4,128)(2,1)} %param.7) | copy-start | bytes 24580
Sparse Core Ops, SparseCore 0:
  75.5 268.8 all-reduce.2
where the time goes:
time: 354 us; the launch traced here: 353 us
  waiting for transfers between devices  312 us (88%)
  between operations  13.4 us (4%)
  local copies, waits for them, and re-layouts  12 us (3%)
  starting transfers between devices  6.94 us (2%)
  matrix products  6.07 us (2%)
    unnamed x2, waiting for transfers between devices  269 us
    all_to_all x1, waiting for transfers between devices, on_device(): lax.all_to_all(amplitudes, 'pair', split_axis=2, concat_axis=0, tiled=True)  43 us
    unnamed x10, local copies, waits for them, and re-layouts  7.48 us
  transfers between devices with their start and end apart: 2, of which 2 were waited for; matrix products, arithmetic and copies ran while one was open for 1% of the time, Pallas kernels for 0%

commit v1 on v0

v1 whole, which is shorter than its diff:
```python
import functools

import jax
import jax.numpy as jnp
from jax import lax
from jax.experimental import pallas as pl
from jax.experimental.pallas import tpu as pltpu
from jax.sharding import PartitionSpec as P

BLK = 64
HALF = 32
MESH = pl.DeviceIdType.MESH
F32, BF16 = jnp.float32, jnp.bfloat16


def tile_parts(q):
    return [[j for j in range(4) if q * j < 4 * t + 4 and q * j + q > 4 * t] for t in range(q)]


def kernel(
    q, a_hbm, i_hbm, bm, o_ref,
    a_v, i_v, pack, recv, sel, part, ybuf, zsend, zbuf, xsend, xbuf,
    a_sem, il_sem, is_sem, ir_sem, as_sem, ar_sem, ys_sem, yr_sem, zs_sem, zr_sem, xs_sem, xr_sem,
):
    pair, slab = lax.axis_index("pair"), lax.axis_index("slab")
    x, h, y, z = pair // 2, pair % 2, slab // 8, slab % 8
    n_groups = a_v.shape[0] // 4
    parts = tile_parts(q)
    first = [0]
    for p in parts:
        first.append(first[-1] + len(p))

    def at_x(d):
        return (lax.rem(x + d, 4) * 2 + h, slab)

    def at_y(d):
        return (pair, lax.rem(y + d, 4) * 8 + z)

    def at_z(d):
        return (pair, y * 8 + lax.rem(z + d, 8))

    other_core = (x * 2 + 1 - h, slab)

    def a_load(g):
        return pltpu.make_async_copy(a_hbm.at[pl.ds(4 * g, 4)], a_v.at[pl.ds(4 * g, 4)], a_sem.at[g])

    rows = pl.ds(pl.multiple_of(80 * h, 16), 80)
    i_local = pltpu.make_async_copy(i_hbm, i_v.at[:, rows], il_sem)
    i_remote = pltpu.make_async_remote_copy(
        i_hbm, i_v.at[:, rows], is_sem, ir_sem, device_id=other_core, device_id_type=MESH)

    for g in range(n_groups):
        a_load(g).start()
    i_local.start()

    barrier = pltpu.get_barrier_semaphore()
    peers = [at_x(d) for d in (1, 2, 3)] + [at_y(d) for d in (1, 2, 3)] + [at_z(d) for d in range(1, 8)]
    peers.append(other_core)
    for peer in peers:
        pl.semaphore_signal(barrier, inc=1, device_id=peer, device_id_type=MESH)

    block0 = (20 * slab) // BLK
    block1 = (20 * slab + 19) // BLK
    row = lax.broadcasted_iota(jnp.int32, (HALF, 128), 0)
    lane = lax.broadcasted_iota(jnp.int32, (HALF, 128), 1)
    diagonal = row == lane % HALF
    lane_unit = lane // HALF

    def build(which, block):
        def one(d, carry):
            k = lax.rem(x + d, 4)
            place = jnp.int32(0)
            for w in range(8):
                inside = jnp.where((w >= k) & (w < k + 5), 1, 0)
                blk = jnp.minimum(2 * k + w // 2, 9)
                ok = bm[block, blk] * inside
                if q == 5:
                    place = w - k
                for t in range(q):
                    for n, j in enumerate(parts[t]):
                        want = jnp.where(ok > 0, place + (q * j - 4 * t), -100)
                        ones = jnp.where(diagonal & (lane_unit == want), 1.0, 0.0).astype(BF16)
                        at = 256 * (first[t] + n) + HALF * w
                        sel[which, d, at:at + HALF, :] = ones
                if q != 5:
                    place = place + ok
            return carry
        lax.fori_loop(0, 4, one, 0)

    build(0, block0)

    @pl.when(block1 != block0)
    def _():
        build(1, block1)

    def pack_one(g, d):
        which = (20 * slab + 4 * g) // BLK - block0
        k = lax.rem(x + d, 4)
        window = pl.ds(pl.multiple_of(128 * k, 128), 256)
        for t in range(q):
            left = jnp.concatenate([a_v[4 * g + j, :, window] for j in parts[t]], axis=1)
            right = sel[which, d, 256 * first[t]:256 * first[t + 1], :]
            pack[d, g, t] = jnp.dot(left, right, preferred_element_type=F32).astype(BF16)

    def a_send(g, d):
        return pltpu.make_async_remote_copy(
            pack.at[d, g], recv.at[d - 1, g], as_sem.at[d - 1, g], ar_sem.at[d - 1, g],
            device_id=at_x(d), device_id_type=MESH)

    pl.semaphore_wait(barrier, len(peers))
    i_remote.start()

    def near(g, carry):
        a_load(g).wait()
        for d in (1, 3):
            pack_one(g, d)
            a_send(g, d).start()
        return carry

    lax.fori_loop(0, n_groups, near, 0)

    def far(g, carry):
        pack_one(g, 2)
        a_send(g, 2).start()
        return carry

    lax.fori_loop(0, n_groups, far, 0)

    def own(g, carry):
        pack_one(g, 0)
        return carry

    lax.fori_loop(0, n_groups, own, 0)
    i_local.wait()
    i_remote.wait()

    def multiply(d, g, held):
        left = jnp.concatenate([held[t] for t in range(q)], axis=1)
        right = i_v[pl.ds(4 * g, 4)].reshape(4 * i_v.shape[1], i_v.shape[2])
        term = jnp.dot(left, right, preferred_element_type=F32)

        @pl.when(g == 0)
        def _():
            part[d] = term

        @pl.when(g > 0)
        def _():
            part[d] += term

    def y_send(d, dy):
        to = lax.rem(y + dy, 4)
        return pltpu.make_async_remote_copy(
            part.at[d, pl.ds(pl.multiple_of(32 * to, 32), 32)], ybuf.at[d, dy - 1],
            ys_sem.at[d, dy - 1], yr_sem.at[d, dy - 1], device_id=at_y(dy), device_id_type=MESH)

    def z_send(d, dz):
        return pltpu.make_async_remote_copy(
            zsend.at[d, lax.rem(z + dz, 8)], zbuf.at[d, dz - 1],
            zs_sem.at[d, dz - 1], zr_sem.at[d, dz - 1], device_id=at_z(dz), device_id_type=MESH)

    def x_send(d):
        return pltpu.make_async_remote_copy(
            xsend.at[d], xbuf.at[d - 1], xs_sem.at[d - 1], xr_sem.at[d - 1],
            device_id=at_x(4 - d), device_id_type=MESH)

    def y_start(d):
        for dy in (2, 1, 3):
            y_send(d, dy).start()

    low = lax.broadcasted_iota(jnp.int32, (8, 512), 0) < 4

    def y_end(d):
        for dy in (1, 2, 3):
            y_send(d, dy).wait_recv()
        base = pl.multiple_of(32 * y, 32)
        for u in range(4):
            total = part[d, pl.ds(base + 8 * u, 8)]
            for dy in (1, 2, 3):
                total = total + ybuf[d, dy - 1, 8 * u:8 * u + 8]
            left, right = total[:, :512], total[:, 512:]
            zsend[d, 2 * u] = jnp.where(low, left, pltpu.roll(right, 4, 0))
            zsend[d, 2 * u + 1] = jnp.where(low, pltpu.roll(left, 4, 0), right)
        for dz in (4, 3, 5, 2, 6, 1, 7):
            z_send(d, dz).start()

    def z_end(d):
        for dz in range(1, 8):
            z_send(d, dz).wait_recv()
        total = zsend[d, z]
        for dz in range(1, 8):
            total = total + zbuf[d, dz - 1]
        xsend[d] = total
        if d:
            x_send(d).start()

    def own_product(g, carry):
        multiply(0, g, pack.at[0, g])
        return carry

    lax.fori_loop(0, n_groups, own_product, 0)
    y_start(0)
    y_end(0)

    def near_product(g, carry):
        for d in (1, 3):
            a_send(g, d).wait_recv()
            multiply(d, g, recv.at[d - 1, g])
        return carry

    lax.fori_loop(0, n_groups, near_product, 0)
    y_start(1)
    y_start(3)
    z_end(0)
    y_end(1)
    y_end(3)

    def far_product(g, carry):
        a_send(g, 2).wait_recv()
        multiply(2, g, recv.at[1, g])
        return carry

    lax.fori_loop(0, n_groups, far_product, 0)
    y_start(2)
    z_end(1)
    z_end(3)
    y_end(2)
    z_end(2)
    for d in (1, 3, 2):
        x_send(d).wait_recv()
    o_ref[...] = (xsend[0] + xbuf[0]) + (xbuf[1] + xbuf[2])

    def sent(g, carry):
        for d in (1, 2, 3):
            a_send(g, d).wait_send()
        return carry

    lax.fori_loop(0, n_groups, sent, 0)
    for d in range(4):
        for dy in (1, 2, 3):
            y_send(d, dy).wait_send()
        for dz in range(1, 8):
            z_send(d, dz).wait_send()
    for d in (1, 2, 3):
        x_send(d).wait_send()


def ladder_call(q, amps, ints, block_map):
    n_c, n_ij, n_d = amps.shape
    n_g = n_c // 4
    dma = pltpu.SemaphoreType.DMA
    return pl.pallas_call(
        functools.partial(kernel, q),
        out_shape=jax.ShapeDtypeStruct((8, 512), F32),
        in_specs=[
            pl.BlockSpec(memory_space=pl.ANY),
            pl.BlockSpec(memory_space=pl.ANY),
            pl.BlockSpec(memory_space=pltpu.SMEM),
        ],
        out_specs=pl.BlockSpec(memory_space=pltpu.VMEM),
        scratch_shapes=[
            pltpu.VMEM((n_c, n_ij, n_d), BF16),
            pltpu.VMEM((n_c, 160, 1024), BF16),
            pltpu.VMEM((4, n_g, q, 128, 128), BF16),
            pltpu.VMEM((3, n_g, q, 128, 128), BF16),
            pltpu.VMEM((2, 4, 256 * sum(map(len, tile_parts(q))), 128), BF16),
            pltpu.VMEM((4, 128, 1024), F32),
            pltpu.VMEM((4, 3, 32, 1024), F32),
            pltpu.VMEM((4, 8, 8, 512), F32),
            pltpu.VMEM((4, 7, 8, 512), F32),
            pltpu.VMEM((4, 8, 512), F32),
            pltpu.VMEM((3, 8, 512), F32),
            dma((n_g,)), dma, dma, dma,
            dma((3, n_g)), dma((3, n_g)),
            dma((4, 3)), dma((4, 3)),
            dma((4, 7)), dma((4, 7)),
            dma((3,)), dma((3,)),
        ],
        compiler_params=pltpu.CompilerParams(
            collective_id=q, has_side_effects=True, vmem_limit_bytes=56 * 2**20),
    )(amps, ints, block_map)


def on_device(amplitudes, integrals, block_map, driver):
    amps = jnp.transpose(amplitudes, (1, 0, 2))
    summed = ladder_call(5, amps, integrals, block_map)
    ladder = jnp.concatenate([summed[:4], summed[4:]], axis=1)
    return driver.astype(F32) + ladder


def solution(mesh):
    placed = (P("pair", "slab", None), P("slab", "pair", None), P(), P(("pair", "slab"), None))
    return jax.shard_map(
        on_device, mesh=mesh, in_specs=placed, out_specs=P(("pair", "slab"), None), check_vma=False
    )
```

time: 354 us -> 66.9 us (0.19)
  waiting for transfers between devices: 312 us -> 0 us
  Pallas kernels: 0 us -> 65.1 us
  between operations: 13.4 us -> 0.01 us
  local copies, waits for them, and re-layouts: 12 us -> 0.8 us
  starting transfers between devices: 6.94 us -> 0 us
  matrix products: 6.07 us -> 0 us
    unnamed x2 -> x0, waiting for transfers between devices: 269 us -> none
    pallas_call x0 -> x1, Pallas kernels: none -> 65.1 us  [ladder_call(): pl.pallas_call(functools.partial(kernel, q), out_shape=jax.ShapeDtypeStru...]
    all_to_all x1 -> x0, waiting for transfers between devices: 43 us -> none  [on_device(): lax.all_to_all(amplitudes, 'pair', split_axis=2, concat_axis=0, tiled=True)]
    unnamed x10 -> x2, local copies, waits for them, and re-layouts: 7.48 us -> 0.01 us
    all_to_all x1 -> x0, starting transfers between devices: 6.93 us -> none  [on_device(): lax.all_to_all(amplitudes, 'pair', split_axis=2, concat_axis=0, tiled=True)]
    dot_general x2 -> x0, matrix products: 6.07 us -> none  [the longest x1 5.69 us: on_device(): jnp.dot(flat_amps, masked, preferred_element_type=jnp.float32)]
    all_to_all x1 -> x0, local copies, waits for them, and re-layouts: 4.37 us -> none  [on_device(): lax.all_to_all(amplitudes, 'pair', split_axis=2, concat_axis=0, tiled=True)]
  transfers between devices with their start and end apart: 2 -> 0, of which waited for: 2 -> 0; matrix products, arithmetic and copies ran while one was open for 1% -> 0% of each run, Pallas kernels for 0% -> 0%
where the time goes in v1:
time: 66.9 us; the launch traced here: 66.5 us
  Pallas kernels  65.1 us (97%)
  local copies, waits for them, and re-layouts  0.8 us (1%)
    pallas_call x1, Pallas kernels, ladder_call(): pl.pallas_call(functools.partial(kernel, q), out_shape=jax.ShapeDtypeStru...  65.1 us

profile of v1, /device:TPU:2, one launch (start us, length us, event | category | flops | bytes accessed | tf_op | source)
XLA Modules:
  0.0 66.5 jit_solution(9988384555467722078)
XLA Ops:
  0.0 0.0 copy-start
  0.0 65.1 %shard_map.46 = f32[8,512]{1,0:T(8,128)} custom-call(bf16[20,128,640]{2,1,0:T(8,128)(2,1)} %bitcast.1, bf16[20,80,1024]{2,1,0:T(8,128)(2,1)} %i_hbm.1, s32[10,10]{1,0:T(8,128)} %bm.1), custom_call_target="tpu_custom_call" | custom-call | tf_op jit(solution)/shard_map/pallas_call | solution.py:251
  65.1 0.8 %fusion = (f32[4,512]{1,0:T(4,128)S(1)}, f32[4,512]{1,0:T(4,128)S(1)}) fusion(f32[8,512]{1,0:T(8,128)} %shard_map.46), kind=kLoop, calls=%fused_computation.1 | loop fusion | bytes 32768 | tf_op jit(solution)/shard_map/slice | solution.py:286
  65.9 0.0 copy-done
  65.9 0.6 maximum_add_fusion
Async XLA Ops:
  0.0 65.9 %copy-start = (bf16[4,1024]{1,0:T(4,128)(2,1)S(1)}, bf16[4,1024]{1,0:T(4,128)(2,1)}, u32[]{:S(2)}) copy-start(bf16[4,1024]{1,0:T(4,128)(2,1)} %param.7) | copy-start | bytes 24580
